TPU v7x, 512 devices: a whole 4x8x8 slice. The times are simulated.
512 devices in a mesh: row: 16 (over z_hi, y), col: 32 (over x, z_lo, core).
Axes of the slice: x: 4, y: 8, z: 8 (z_hi: 2, z_lo: 4; z = z_hi * 4 + z_lo), core: 2. Of those that a mesh axis runs over, the one named last changes fastest.
Arguments:
- cov_tiles: float32 [2, 16, 1, 32, 512, 512], P(None, 'row', None, 'col'), may hold values from -6 to 6
- inverse_factors: float32 [2, 512, 512], P(None, 'row'), may hold values from -0.3 to 0.3, as said below
- band: int32 [32], replicated, may hold values from 1 to 24, as said below
- station_noise: float32 [16384], replicated, may hold values from 0.5 to 4
- morton: int32 [16384], replicated, may hold values from 0 to 16383, each once
Outputs:
- factor_window: float32 [2, 16, 1, 32, 512, 512], P(None, 'row', None, 'col')
Inputs may be any that keep to these rules, and one draw needn't show every extreme that they name: `inverse_factors`: each matrix is upper triangular with a positive diagonal. Some row of tiles has a band of exactly 24.
All inputs are finite; a program needn't handle non-finite values.
Results may differ from a plain program's by a relative error of at most 0.0003.
Values sent between devices are 32-bit elements; how exact they have to be, the bound alone decides.
A program may use at most 64 MiB of HBM per device.

v0:
```python
import jax
import jax.numpy as jnp
from jax import lax
from jax.sharding import PartitionSpec as P

STEPS = 2


def spread(value, axis, source):
    kept = jnp.where(lax.axis_index(axis) == source, value, 0).astype(value.dtype)
    return lax.psum(kept, axis)


def on_device(cov_tiles, inverse_factors, band, station_noise, morton):
    grid_rows = lax.axis_size("row")
    grid_cols = lax.axis_size("col")
    own_row = lax.axis_index("row")
    own_col = lax.axis_index("col")
    blocks = cov_tiles[:, 0, :, 0]
    tile_rows = blocks.shape[0]
    tile_cols = blocks.shape[1]
    tile_size = blocks.shape[2]
    tile_count = band.shape[0]
    row_ids = jnp.arange(tile_rows, dtype=jnp.int32) * grid_rows + own_row
    col_ids = jnp.arange(tile_cols, dtype=jnp.int32) * grid_cols + own_col
    every_tile = jnp.arange(tile_count, dtype=jnp.int32)
    row_band = jnp.sum(jnp.where(every_tile[None, :] == row_ids[:, None], band[None, :], 0), axis=1)
    kept_mask = (col_ids[None, :] <= row_ids[:, None]) & (
        row_ids[:, None] - col_ids[None, :] <= row_band[:, None]
    )
    blocks = jnp.where(kept_mask[:, :, None, None], blocks, 0.0)
    is_diagonal = col_ids[None, :] == row_ids[:, None]
    mirrored = jnp.tril(blocks) + jnp.swapaxes(jnp.tril(blocks, -1), -1, -2)
    station_rows = morton.reshape(tile_count, tile_size)[row_ids]
    nugget = station_noise[station_rows]
    identity = jnp.eye(tile_size, dtype=jnp.float32)
    mirrored = mirrored + nugget[:, None, :, None] * identity
    blocks = jnp.where(is_diagonal[:, :, None, None], mirrored, blocks)
    for panel_step in range(STEPS):
        factor = lax.all_gather(inverse_factors[panel_step], "row", axis=0, tiled=True)
        owner_col = panel_step % grid_cols
        owner_slot = panel_step // grid_cols

        def make_factor(column):
            return jnp.einsum(
                "amn,np->amp",
                column,
                factor,
                precision=lax.Precision.HIGHEST,
                preferred_element_type=jnp.float32,
            )

        column = blocks[:, owner_slot]
        row_factor = lax.cond(own_col == owner_col, make_factor, jnp.zeros_like, column)
        row_factor = jnp.where((row_ids > panel_step)[:, None, None], row_factor, 0.0)
        row_factor = spread(row_factor, "col", owner_col)
        blocks = blocks.at[:, owner_slot].set(jnp.where(own_col == owner_col, row_factor, column))
        target = 0 + own_col
        held_tile = lax.dynamic_index_in_dim(row_factor, target // grid_rows, 0, keepdims=False)
        pieces = [spread(held_tile, "row", target % grid_rows)]
        col_factor = jnp.stack(pieces)
        update = jnp.einsum(
            "amp,bnp->abmn",
            row_factor,
            col_factor,
            precision=lax.Precision.HIGHEST,
            preferred_element_type=jnp.float32,
        )
        active = (col_ids[None, :] > panel_step) & (col_ids[None, :] <= row_ids[:, None])
        blocks = blocks - jnp.where(active[:, :, None, None], update, 0.0)
    return blocks[:, None, :, None]


def solution(mesh):
    placed = (P(None, "row", None, "col", None, None), P(None, "row", None), P(), P(), P())
    return jax.shard_map(
        on_device,
        mesh=mesh,
        in_specs=placed,
        out_specs=P(None, "row", None, "col", None, None),
        check_vma=False,
    )
```

profile of v0, /device:TPU:2, one launch (start us, length us, event | category | flops | bytes accessed | tf_op | source)
XLA Modules:
  0.0 1189.5 jit_solution(2500794160252668181)
XLA Ops:
  6.5 0.0 copy-start
  6.5 0.0 all-gather.5.cloned.1.call-start
  6.5 1.6 fusion.13
  8.1 0.0 all-gather.5.cloned.1.call-update
  8.1 0.0 all-reduce.5.cloned.1.call-start
  8.2 0.8 fusion.11
  9.1 1.9 bitcast_select_fusion.2
  11.0 0.0 copy-start.4
  11.0 1.8 copy.21
  12.8 0.0 copy-done.4
  12.8 0.6 gather_fusion
  13.4 0.0 copy-done
  13.4 0.0 copy-start.1
  13.4 6.2 gather_fusion.1
  19.6 0.2 iota_compare_fusion.2
  19.8 0.2 iota_compare_fusion.1
  20.1 0.0 copy-done.1
  20.1 3.7 fusion.6
  23.7 2.9 copy.23
  26.7 3.5 select_bitcast_fusion
  30.1 78.5 %all-gather.5.cloned.1.call-done = f32[1,512,512]{2,1,0:T(8,128)} async-done(((f32[1,32,512]{2,1,0:T(8,128)}), f32[1,512,512]{2,1,0:T(8,128)}) %all-gather.5.cloned.1.call-update) | async-done | bytes 1048592 | tf_op jit(solution)/shard_map/all_gather | solution.py:40
  108.6 0.3 conditional.2
  108.6 0.2 broadcast.314
  108.9 1.7 select_select_fusion.1
  110.6 0.0 all-reduce.5.cloned.1.call-update
  110.6 0.0 copy-start.2
  110.6 0.0 all-reduce.7.cloned.1.call-start
  110.7 269.9 %all-reduce.5.cloned.1.call-done = f32[2,512,512]{2,1,0:T(8,128)} async-done(((f32[2,512,512]{2,1,0:T(8,128)}), f32[2,512,512]{2,1,0:T(8,128)}) %all-reduce.5.cloned.1.call-update) | async-done | bytes 2097168 | tf_op jit(solution)/shard_map/psum | solution.py:11
  380.6 2.3 select_bitcast_fusion.2
  382.9 0.0 all-reduce.7.cloned.1.call-update
  382.9 0.0 all-gather.7.cloned.1.call-start
  383.0 0.5 all-gather.7.cloned.1.call-update
  383.5 0.0 all-reduce.9.cloned.1.call-start
  383.6 211.9 %all-reduce.7.cloned.1.call-done = f32[512,512]{1,0:T(8,128)} async-done(((f32[512,512]{1,0:T(8,128)}), f32[512,512]{1,0:T(8,128)}) %all-reduce.7.cloned.1.call-update) | async-done | bytes 1048592 | tf_op jit(solution)/shard_map/psum | solution.py:11
  595.5 7.4 fusion.5
  602.9 86.3 %all-gather.7.cloned.1.call-done = f32[1,512,512]{2,1,0:T(8,128)} async-done(((f32[1,32,512]{2,1,0:T(8,128)}), f32[1,512,512]{2,1,0:T(8,128)}) %all-gather.7.cloned.1.call-update) | async-done | bytes 1048592 | tf_op jit(solution)/shard_map/all_gather | solution.py:40
  689.2 0.4 conditional.3
  689.2 0.2 broadcast.315
  689.7 1.7 select_select_fusion
  691.4 0.0 all-reduce.9.cloned.1.call-update
  691.4 0.0 copy-start.3
  691.5 0.0 all-reduce.11.cloned.1.call-start
  691.5 268.7 %all-reduce.9.cloned.1.call-done = f32[2,512,512]{2,1,0:T(8,128)} async-done(((f32[2,512,512]{2,1,0:T(8,128)}), f32[2,512,512]{2,1,0:T(8,128)}) %all-reduce.9.cloned.1.call-update) | async-done | bytes 2097168 | tf_op jit(solution)/shard_map/psum | solution.py:11
  960.3 2.3 select_bitcast_fusion.1
  962.6 0.0 all-reduce.11.cloned.1.call-update
  962.6 212.6 %all-reduce.11.cloned.1.call-done = f32[512,512]{1,0:T(8,128)} async-done(((f32[512,512]{1,0:T(8,128)}), f32[512,512]{1,0:T(8,128)}) %all-reduce.11.cloned.1.call-update) | async-done | bytes 1048592 | tf_op jit(solution)/shard_map/psum | solution.py:11
  1175.2 0.0 copy-done.3
  1175.2 7.4 fusion.4
  (15 shorter events, 0.1 us)
Async XLA Ops:
  6.5 6.9 copy-start
  6.5 102.1 %all-gather.5.cloned.1.call-start = ((), (), s32[]{:S(2)}) async-start(), calls=%async_computation.4 | async-start | bytes 1114112 | tf_op jit(solution)/shard_map/all_gather | solution.py:40
  8.1 372.5 %all-reduce.5.cloned.1.call-start = ((), (), s32[]{:S(2)}) async-start(), calls=%async_computation | async-start | bytes 4194304 | tf_op jit(solution)/shard_map/psum | solution.py:11
  11.0 1.8 copy-start.4
  13.4 6.6 copy-start.1
  110.6 484.9 %copy-start.2 = (f32[2,512,512]{2,1,0:T(8,128)S(1)}, f32[2,512,512]{2,1,0:T(8,128)}, u32[]{:S(2)}) copy-start(f32[2,512,512]{2,1,0:T(8,128)} %select_bitcast_fusion) | copy-start | bytes 6291460
  110.6 484.9 %all-reduce.7.cloned.1.call-start = ((), (), s32[]{:S(2)}) async-start(), calls=%async_computation.1 | async-start | bytes 2097152 | tf_op jit(solution)/shard_map/psum | solution.py:11
  382.9 306.3 %all-gather.7.cloned.1.call-start = ((), (), s32[]{:S(2)}) async-start(), calls=%async_computation.5 | async-start | bytes 1114112 | tf_op jit(solution)/shard_map/all_gather | solution.py:40
  383.5 576.7 %all-reduce.9.cloned.1.call-start = ((), (), s32[]{:S(2)}) async-start(), calls=%async_computation.2 | async-start | bytes 4194304 | tf_op jit(solution)/shard_map/psum | solution.py:11
  691.4 483.8 %copy-start.3 = (f32[2,512,512]{2,1,0:T(8,128)S(1)}, f32[2,512,512]{2,1,0:T(8,128)}, u32[]{:S(2)}) copy-start(f32[2,512,512]{2,1,0:T(8,128)} %fusion.5) | copy-start | bytes 6291460
  691.5 483.8 %all-reduce.11.cloned.1.call-start = ((), (), s32[]{:S(2)}) async-start(), calls=%async_computation.3 | async-start | bytes 2097152 | tf_op jit(solution)/shard_map/psum | solution.py:11
Sparse Core Ops, SparseCore 0:
  10.6 97.9 all-gather.4
  111.5 269.0 all-reduce.4
  383.8 211.6 all-reduce.6
  598.6 90.6 all-gather.6
  692.0 268.2 all-reduce.8
  963.3 211.8 all-reduce.10
where the time goes:
time: 1190 us
  waiting for transfers between devices  1130 us (95%)
  other arithmetic  18.4 us (2%)
  matrix products  14.8 us (1%)
  between operations  13.7 us (1%)
  local copies, waits for them, and re-layouts  13.5 us (1%)
    psum x4, waiting for transfers between devices, spread(): return lax.psum(kept, axis)  963 us
    all_gather x2, waiting for transfers between devices, on_device(): lax.all_gather(inverse_factors[panel_step], 'row', axis=0, tiled=True)  165 us
  transfers between devices with their start and end apart: 6, of which 6 were waited for; matrix products, arithmetic and copies ran while one was open for 2% of the time, Pallas kernels for 0%

commit v1 on v0

v1 whole, which is shorter than its diff:
```python
import jax
import jax.numpy as jnp
from jax import lax
from jax.experimental import pallas as pl
from jax.experimental.pallas import tpu as pltpu
from jax.sharding import PartitionSpec as P

TILE = 512
NP = 16
PIECE = 2 * TILE // NP
HALF = PIECE // 2
ROW_HOP = 2
COL_HOP = 2
DEEPEST = 9
STEPS = NP + ROW_HOP * DEEPEST + COL_HOP * 7 + 1
BLOCK = 128
MESH = pl.DeviceIdType.MESH
F32 = jnp.float32
BF16 = jnp.bfloat16


def device(x, y, z, core):
    x, y, z = lax.rem(x + 4, 4), lax.rem(y + 8, 8), lax.rem(z + 8, 8)
    return (z // 4 * 8 + y, x * 8 + z % 4 * 2 + core)


def split(value):
    high = value.astype(BF16)
    return high, (value - high.astype(F32)).astype(BF16)


def dot3(a, b, transposed):
    dims = (((1,), (1 if transposed else 0,)), ((), ()))

    def dot(p, q):
        return lax.dot_general(p, q, dims, preferred_element_type=F32)

    return dot(a[0], b[0]) + (dot(a[0], b[1]) + dot(a[1], b[0]))


def either(*conditions):
    result = conditions[0]
    for condition in conditions[1:]:
        result = result | condition
    return result


def count(*conditions):
    return sum(jnp.where(condition, 1, 0) for condition in conditions)


def kernel(cov, factors, band, noise, morton, out, buf, panel, fac, lead, wide, narrow,
           row_got, side_got, up_got, down_got, fac_got, lead_got, one_got,
           z_sent, xp_sent, xm_sent, side_sent, cross_sent, up_sent, down_sent, fac_sent, lead_sent, spread_sent, one_sent):
    row = lax.axis_index("row")
    col = lax.axis_index("col")
    half, y = row // 8, row % 8
    x, zl, core = col // 8, col % 8 // 2, col % 2
    z = half * 4 + zl
    other = 1 - core
    sibling = device(x, y, z, other)
    home = (x == 0) & (zl == 0)
    first, second = core == 0, core == 1
    low, high = half == 0, half == 1
    tail = high & (y <= 1)

    z_child = (zl < 3) & either(first & (x == 0), second & low & (x == 1), second & tail & (x == 2))
    xp_child = either(first & high & (x == 0), second & low & either(x == 1, home))
    xm_child = either(second & low & (x == 1) & (zl >= 1),
                      second & tail & either(home, (x == 3) & (zl == 0), x == 2, (x == 1) & (zl >= 1)))
    from_z = (zl >= 1) & either(first & (x == 0), second & low & (x == 1), second & tail & (x == 2))
    from_xm = either(first & high & (x == 1), second & low & either(x == 2, (x == 1) & (zl == 0)))
    from_xp = either(second & low & (x == 0) & (zl >= 1),
                     second & tail & either((x == 3) & (zl == 0), (x == 2) & (zl == 0), x == 1, (x == 0) & (zl >= 1)))
    row_in = either(from_z, from_xm, from_xp)
    has_row = home | row_in
    side_in = home | either(second & ((x == 0) | (high & (x == 1))),
                            first & low & (x <= 2),
                            first & tail & ((x <= 2) | (zl == 0)))
    depth_low = jnp.where(x == 1, zl + 1, zl + 2)
    depth_tail = jnp.where(x == 3, 1, zl + jnp.where(x == 2, 2, jnp.where(x == 1, 3, 4)))
    depth = jnp.where(home, 0, jnp.where(first, zl + x, jnp.where(low, depth_low, depth_tail)))

    place = lax.rem(y - 2 * zl - core + 8, 8)
    ring = (x <= 2) & jnp.logical_not(home)
    source = ring & (place == 0)
    follower = ring & (place >= 1)
    own_row = source & either((x == half), (x == 2) & low)
    crossed = source & jnp.logical_not(own_row)
    last = (x == 3) & (zl == 0) & high & first
    last_source, last_follower = last & (y == 0), last & (y == 1)
    slot = jnp.where(x >= 2, 1, 0)
    by_side = (own_row & (slot != core)) | last_source
    lag = jnp.where(x == 3, 3,
                    jnp.where(x == 2, zl + 3 + 2 * half,
                              jnp.where(x == half, zl + x + core, 2)))
    held = jnp.where(either(own_row, (x == 3) & (zl == 0) & high & jnp.logical_not(last_follower)), slot, 2)
    cross_out = home & first & jnp.logical_not(low & (y < 2))
    jump_out = (x == 2) & low & (place == 0)
    jump_in = (x == 2) & high & (place == 0)
    cross_in = crossed & (x <= 1)
    send_up = (ring & (place <= 6))
    send_down = (ring & (place != 1))

    fac_own = home & first
    fac_far = (x == 0) & (zl == 3) & second
    fac_next = (x == 1) & (zl == 0) & first
    fac_off = (x == 3) & (zl == 3) & second
    scatter = home & low & (y == 1) & first
    relay = low & (y == 1) & (core == zl % 2)
    relay_place = zl % 2 * 8 + x * 2 + zl // 2

    barrier = pltpu.get_barrier_semaphore()

    def greet(target):
        pl.semaphore_signal(barrier, inc=1, device_id=target, device_id_type=MESH)

    def greet_if(condition, target):
        @pl.when(condition)
        def _():
            greet(target)

    greet(sibling)

    @pl.when(home)
    def _():
        for step in range(8):
            @pl.when(first)
            def _():
                @pl.when(y != step)
                def _():
                    greet(device(0, step, z, 0))

                greet(device(1, step, z, 0))

            @pl.when(second)
            def _():
                greet(device(0, step, z + 7, 1))
                greet(device(3, step, z + 7, 1))

            @pl.when(jnp.logical_not(scatter & (step == 0)))
            def _():
                greet(device(step // 2, 1, step % 2 * 2 + core, core))

    greet_if(relay & jnp.logical_not(scatter), device(0, 1, 0, 0))
    greet_if(from_z, device(x, y, z + 7, core))
    greet_if(from_xm, device(x + 3, y, z, core))
    greet_if(from_xp, device(x + 1, y, z, core))
    greet_if(follower, device(x, y + 7, z, core))
    greet_if(follower, device(x, y + 1, z, core))
    greet_if(last_follower, device(x, y + 7, z, core))
    greet_if(cross_in, device(0, y, 4 - 4 * half, 0))
    greet_if(jump_in, device(2, y, zl, core))
    targets = 1 + count(z_child, xp_child, xm_child, send_up, send_down, last_source, cross_out, jump_out)
    targets = targets + 7 * count(fac_own) + 8 * count(fac_far, fac_next, fac_off)
    targets = targets + 16 * count(relay) + 14 * count(scatter)
    pl.semaphore_wait(barrier, targets)

    def remote(src, dst, sent, got, target):
        return pltpu.make_async_remote_copy(
            src_ref=src, dst_ref=dst, send_sem=sent, recv_sem=got, device_id=target, device_id_type=MESH
        )

    chunk = TILE // 16

    def fac_rows(source_row):
        return pl.ds(pl.multiple_of(source_row * chunk, chunk), chunk)

    def fac_copy(part, step, target):
        return remote(factors.at[part], fac.at[part, fac_rows(row)], fac_sent.at[step], fac_got.at[part, y], target)

    def send_factors(condition, part, target_x, target_z, target_core, skip_self):
        @pl.when(condition)
        def _():
            for step in range(8):
                target = device(target_x, step, target_z, target_core)
                if skip_self:
                    @pl.when(y != step)
                    def _():
                        fac_copy(part, step, target).start()
                else:
                    fac_copy(part, step, target).start()

    def drain_factors(condition, part, skip_self):
        @pl.when(condition)
        def _():
            for step in range(8):
                if skip_self:
                    @pl.when(y != step)
                    def _():
                        fac_copy(part, step, sibling).wait_send()
                else:
                    fac_copy(part, step, sibling).wait_send()

    send_factors(fac_own, 0, 0, z, 0, True)
    send_factors(fac_far, 0, 0, z + 1, 1, False)
    side_panel = remote(cov.at[other], panel.at[core], one_sent.at[0], one_got.at[0], sibling)

    def lead_rows(number):
        return pl.ds(pl.multiple_of(number * chunk, chunk), chunk)

    def scatter_copy(number):
        parity, sx, sz = number // 8, number % 8 // 2, number % 2
        rows = pl.ds(number * chunk, chunk)
        return remote(cov.at[0, rows], lead.at[rows], spread_sent.at[number], one_got.at[4],
                      device(sx, 1, sz * 2 + parity, parity))

    @pl.when(scatter)
    def _():
        for number in range(1, 16):
            scatter_copy(number).start()
        lead[pl.ds(0, chunk)] = cov[0, pl.ds(0, chunk)]

    @pl.when(home)
    def _():
        side_panel.start()

    send_factors(fac_next, 1, 0, z, 0, False)
    send_factors(fac_off, 1, 0, z + 1, 1, False)

    def lead_copy(number, target):
        rows = lead_rows(relay_place)
        return remote(lead.at[rows], lead.at[rows], lead_sent.at[number], lead_got.at[relay_place % 8], target)

    @pl.when(relay)
    def _():
        rows = lead_rows(relay_place)

        @pl.when(jnp.logical_not(scatter))
        def _():
            remote(lead.at[rows], lead.at[rows], one_sent.at[4], one_got.at[4], sibling).wait_recv()

        for number in range(16):
            @pl.when(jnp.logical_not(scatter & (number == 1)))
            def _():
                lead_copy(number, device(0, number % 8, number // 8 * 4, core)).start()

    side_fac = [
        remote(fac.at[part, pl.ds(pl.multiple_of(jnp.where(first, half, 1 - half) * 256, 256), 256)],
               fac.at[part, pl.ds(pl.multiple_of(jnp.where(first, half, 1 - half) * 256, 256), 256)],
               one_sent.at[1 + part], one_got.at[1 + part], sibling)
        for part in range(2)
    ]
    side_lead_rows = pl.ds(pl.multiple_of(core * 256, 256), 256)
    side_lead = remote(lead.at[side_lead_rows], lead.at[side_lead_rows], one_sent.at[3], one_got.at[3], sibling)

    def wait_factors(part):
        own = jnp.where(first, half, 1 - half)
        if part == 0:
            @pl.when(first)
            def _():
                fac[0, fac_rows(row)] = factors[0]

        for step in range(8):
            def wait(step=step):
                remote(factors.at[part], fac.at[part, fac_rows(own * 8 + step)], fac_sent.at[step],
                       fac_got.at[part, step], sibling).wait_recv()

            if part == 0:
                pl.when(jnp.logical_not(first & (y == step)))(wait)
            else:
                wait()
        side_fac[part].start()

    def wait_lead():
        for step in range(8):
            @pl.when(jnp.logical_not(scatter & (step == 0)))
            def _():
                rows = lead_rows(core * 8 + step)
                remote(lead.at[rows], lead.at[rows], lead_sent.at[step], lead_got.at[step], sibling).wait_recv()
        side_lead.start()

    blocks = TILE // BLOCK

    def block_rows(number, start=0):
        return pl.ds(pl.multiple_of(start + number * BLOCK, BLOCK), BLOCK)

    def split_into(place, load):
        def body(number, carry):
            rows = block_rows(number)
            wide[place, rows], narrow[place, rows] = split(load(rows))
            return carry

        lax.fori_loop(0, blocks, body, 0)

    tile_row = core * 16 + row
    row_band = band[tile_row]

    def make_first():
        wait_factors(0)
        side_panel.wait_recv()

        @pl.when(first)
        def _():
            panel[0] = cov[0]

        @pl.when(second)
        def _():
            panel[1] = cov[1]

        side_fac[0].wait_recv()
        split_into(0, lambda rows: fac[0, rows])
        kept = (tile_row > 0) & (tile_row <= row_band)

        def body(number, carry):
            rows = block_rows(number)
            left = split(jnp.where(kept, panel[0, rows], 0.0))
            buf[core, rows] = dot3(left, (wide[0], narrow[0]), False)
            return carry

        lax.fori_loop(0, blocks, body, 0)

    def make_second():
        wait_factors(1)
        wait_lead()
        side_fac[1].wait_recv()
        side_lead.wait_recv()
        split_into(2, lambda rows: fac[1, rows])
        lead_kept = band[1] >= 1

        def body_lead(number, carry):
            rows = block_rows(number)
            left = split(jnp.where(lead_kept, lead[rows], 0.0))
            wide[1, rows], narrow[1, rows] = split(dot3(left, (wide[0], narrow[0]), False))
            return carry

        lax.fori_loop(0, blocks, body_lead, 0)
        kept = (tile_row > 0) & (tile_row - 1 <= row_band)

        def body(number, carry):
            rows = block_rows(number)
            update = dot3(split(buf[core, rows]), (wide[1], narrow[1]), True)
            left = split(jnp.where(kept, panel[1, rows], 0.0) - update)
            made = dot3(left, (wide[2], narrow[2]), False)
            buf[core, block_rows(number, TILE)] = jnp.where(tile_row > 1, made, 0.0)
            return carry

        lax.fori_loop(0, blocks, body, 0)

    def make_base():
        diagonal = row == lax.rem(col, 16)
        for s in range(2):
            tile = s * 16 + row
            kept = (col <= tile) & (tile - col <= band[tile])
            on_diagonal = diagonal & (col // 16 == s)

            @pl.when(on_diagonal)
            def _():
                stations = morton[pl.ds(tile, 1), :]
                upper, lower = stations // 128, stations % 128
                lanes = lax.broadcasted_iota(jnp.int32, (128, TILE), 0)
                pick = jnp.where(lanes == upper, 1.0, 0.0).astype(BF16)
                values = noise[...].T
                top = values.astype(BF16)
                rest = values - top.astype(F32)
                middle = rest.astype(BF16)
                bottom = (rest - middle.astype(F32)).astype(BF16)
                found = jnp.dot(top, pick, preferred_element_type=F32)
                found = found + (jnp.dot(middle, pick, preferred_element_type=F32)
                                 + jnp.dot(bottom, pick, preferred_element_type=F32))
                nugget = jnp.sum(jnp.where(lanes == lower, found, 0.0), axis=0, keepdims=True)
                for number in range(blocks):
                    at = number * BLOCK
                    rows_at = lax.broadcasted_iota(jnp.int32, (BLOCK, TILE), 0) + at
                    cols_at = lax.broadcasted_iota(jnp.int32, (BLOCK, TILE), 1)
                    here = cov[s, pl.ds(at, BLOCK), :]
                    turned = cov[s, :, pl.ds(at, BLOCK)].T
                    value = jnp.where(cols_at <= rows_at, here, turned)
                    out[s, pl.ds(at, BLOCK), :] = value + jnp.where(rows_at == cols_at, nugget, 0.0)

            @pl.when(jnp.logical_not(on_diagonal))
            def _():
                def body(number, carry):
                    rows = block_rows(number)
                    out[s, rows] = jnp.where(kept, cov[s, rows], 0.0)
                    return carry

                lax.fori_loop(0, blocks, body, 0)

    pl.when(home)(make_first)
    pl.when(jnp.logical_not(home))(make_base)

    def piece(index):
        return pl.ds(pl.multiple_of(index * PIECE, PIECE), PIECE)

    def half_piece(index, which):
        return pl.ds(pl.multiple_of(index * PIECE + which * HALF, HALF), HALF)

    def row_copy(index, sent, target):
        rows = piece(index)
        return remote(buf.at[core, rows], buf.at[core, rows], sent.at[index], row_got.at[index], target)

    def side_copy(index):
        rows = piece(index)
        return remote(buf.at[core, rows], buf.at[core, rows], side_sent.at[index], side_got.at[index], sibling)

    def side_arrival(index):
        rows = piece(index)
        return remote(buf.at[other, rows], buf.at[other, rows], side_sent.at[index], side_got.at[index], sibling)

    def whole_copy(index, from_slot, sent, target):
        rows = piece(index)
        return remote(buf.at[from_slot, rows], buf.at[2, rows], sent.at[index], up_got.at[index], target)

    def ring_copy(index, which, sent, got, target):
        rows = half_piece(index, which)
        return remote(buf.at[held, rows], buf.at[2, rows], sent.at[index], got.at[index], target)

    z_to, xp_to, xm_to = device(x, y, z + 1, core), device(x + 1, y, z, core), device(x + 3, y, z, core)
    up_to, down_to = device(x, y + 1, z, core), device(x, y + 7, z, core)
    cross_to = device(half, y, (1 - half) * 4 + y // 2, y % 2)
    jump_to = device(2, y, 4 + zl, core)
    row_delay = depth * ROW_HOP
    col_delay = lag * ROW_HOP

    def inside(index):
        return (index >= 0) & (index < NP)

    def step(time, carry):
        index = time - row_delay

        @pl.when(has_row & inside(index))
        def _():
            pl.when(home & (index == NP // 2))(make_second)

            @pl.when(row_in)
            def _():
                row_copy(index, z_sent, z_to).wait_recv()

            @pl.when(z_child)
            def _():
                row_copy(index, z_sent, z_to).start()

            @pl.when(xp_child)
            def _():
                row_copy(index, xp_sent, xp_to).start()

            @pl.when(xm_child)
            def _():
                row_copy(index, xm_sent, xm_to).start()

            @pl.when(cross_out)
            def _():
                whole_copy(index, 0, cross_sent, cross_to).start()

            side_copy(index).start()

        ahead = time - col_delay

        @pl.when((source | last_source) & inside(ahead))
        def _():
            @pl.when(by_side)
            def _():
                side_arrival(ahead).wait_recv()

            @pl.when(crossed)
            def _():
                whole_copy(ahead, 2, up_sent, up_to).wait_recv()

            @pl.when(source)
            def _():
                ring_copy(ahead, 0, up_sent, up_got, up_to).start()
                ring_copy(ahead, 1, down_sent, down_got, down_to).start()

            @pl.when(jump_out)
            def _():
                whole_copy(ahead, 1, cross_sent, jump_to).start()

            @pl.when(last_source)
            def _():
                whole_copy(ahead, 1, up_sent, up_to).start()

        going_up = ahead - COL_HOP * place
        going_down = ahead - COL_HOP * (8 - place)

        @pl.when(follower & inside(going_up))
        def _():
            copy = ring_copy(going_up, 0, up_sent, up_got, up_to)
            copy.wait_recv()

            @pl.when(place <= 6)
            def _():
                copy.start()

        @pl.when(follower & inside(going_down))
        def _():
            copy = ring_copy(going_down, 1, down_sent, down_got, down_to)
            copy.wait_recv()

            @pl.when(place >= 2)
            def _():
                copy.start()

        return carry

    lax.fori_loop(0, STEPS, step, 0)

    def finish(index, carry):
        @pl.when(side_in & jnp.logical_not(by_side))
        def _():
            side_arrival(index).wait_recv()

        @pl.when(last_follower)
        def _():
            whole_copy(index, 2, up_sent, up_to).wait_recv()

        return carry

    lax.fori_loop(0, NP, finish, 0)

    @pl.when(home)
    def _():
        for s in range(2):
            def body(number, carry):
                rows = block_rows(number)
                out[s, rows] = buf[s, block_rows(number, core * TILE)]
                return carry

            lax.fori_loop(0, blocks, body, 0)

    needed = [jnp.logical_not(home) & (col <= s * 16 + row) & (s * 16 + row <= 25) for s in range(2)]

    @pl.when(needed[0] | needed[1])
    def _():
        for part in range(2):
            split_into(part, lambda rows: buf[held, pl.ds(pl.multiple_of(rows.start + part * TILE, BLOCK), BLOCK)])
        for s in range(2):
            @pl.when(needed[s])
            def _():
                def body(number, carry):
                    rows = block_rows(number)
                    total = out[s, rows]
                    for part in range(2):
                        left = split(buf[s, block_rows(number, part * TILE)])
                        total = total - dot3(left, (wide[part], narrow[part]), True)
                    out[s, rows] = total
                    return carry

                lax.fori_loop(0, blocks, body, 0)

    def drain(index, carry):
        @pl.when(z_child)
        def _():
            row_copy(index, z_sent, z_to).wait_send()

        @pl.when(xp_child)
        def _():
            row_copy(index, xp_sent, xp_to).wait_send()

        @pl.when(xm_child)
        def _():
            row_copy(index, xm_sent, xm_to).wait_send()

        @pl.when(has_row)
        def _():
            side_copy(index).wait_send()

        @pl.when(cross_out | jump_out)
        def _():
            whole_copy(index, 2, cross_sent, cross_to).wait_send()

        @pl.when(last_source)
        def _():
            whole_copy(index, 1, up_sent, up_to).wait_send()

        @pl.when(send_up)
        def _():
            ring_copy(index, 0, up_sent, up_got, up_to).wait_send()

        @pl.when(send_down)
        def _():
            ring_copy(index, 1, down_sent, down_got, down_to).wait_send()

        return carry

    lax.fori_loop(0, NP, drain, 0)
    drain_factors(fac_own, 0, True)
    drain_factors(fac_far, 0, False)
    drain_factors(fac_next, 1, False)
    drain_factors(fac_off, 1, False)

    @pl.when(scatter)
    def _():
        for number in range(1, 16):
            scatter_copy(number).wait_send()

    @pl.when(relay)
    def _():
        for number in range(16):
            @pl.when(jnp.logical_not(scatter & (number == 1)))
            def _():
                lead_copy(number, sibling).wait_send()

    @pl.when(home)
    def _():
        side_panel.wait_send()
        side_fac[0].wait_send()
        side_fac[1].wait_send()
        side_lead.wait_send()


def on_device(cov_tiles, inverse_factors, band, station_noise, morton):
    vmem = pl.BlockSpec(memory_space=pltpu.VMEM)
    smem = pl.BlockSpec(memory_space=pltpu.SMEM)
    dma = pltpu.SemaphoreType.DMA
    out = pl.pallas_call(
        kernel,
        out_shape=jax.ShapeDtypeStruct((2, TILE, TILE), F32),
        in_specs=[vmem, vmem, smem, vmem, vmem],
        out_specs=vmem,
        scratch_shapes=[
            pltpu.VMEM((3, 2 * TILE, TILE), F32),
            pltpu.VMEM((2, TILE, TILE), F32),
            pltpu.VMEM((2, TILE, TILE), F32),
            pltpu.VMEM((TILE, TILE), F32),
            pltpu.VMEM((3, TILE, TILE), BF16),
            pltpu.VMEM((3, TILE, TILE), BF16),
            dma((NP,)), dma((NP,)), dma((NP,)), dma((NP,)), dma((2, 8)), dma((8,)), dma((5,)),
            dma((NP,)), dma((NP,)), dma((NP,)), dma((NP,)), dma((NP,)), dma((NP,)), dma((NP,)),
            dma((8,)), dma((16,)), dma((16,)), dma((5,)),
        ],
        compiler_params=pltpu.CompilerParams(
            collective_id=0, has_side_effects=True, vmem_limit_bytes=40 * 1024 * 1024
        ),
        cost_estimate=pl.CostEstimate(flops=6 * 4 * 2 * TILE**3, bytes_accessed=4 * 1024 * 1024, transcendentals=0),
        name="panel_steps",
    )(
        cov_tiles.reshape(2, TILE, TILE),
        inverse_factors,
        band,
        station_noise.reshape(128, 128),
        morton.reshape(32, TILE),
    )
    return out.reshape(cov_tiles.shape)


def solution(mesh):
    placed = (P(None, "row", None, "col", None, None), P(None, "row", None), P(), P(), P())
    return jax.shard_map(
        on_device,
        mesh=mesh,
        in_specs=placed,
        out_specs=P(None, "row", None, "col", None, None),
        check_vma=False,
    )
```

time: 1190 us -> 114 us (0.10)
  the two profiles are of different devices: /device:TPU:2 before, /device:TPU:10 now
where the time goes in v1:
time: 114 us
  Pallas kernels  108 us (95%)
  local copies, waits for them, and re-layouts  6.16 us (5%)
    pallas_call x1, Pallas kernels, on_device(): pl.pallas_call(kernel, out_shape=jax.ShapeDtypeStruct((2, TILE, TILE), F3...  108 us
    unnamed x9, local copies, waits for them, and re-layouts  5.31 us

profile of v1, /device:TPU:10, one launch (start us, length us, event | category | flops | bytes accessed | tf_op | source)
XLA Modules:
  0.0 114.0 jit_solution(1495760583867390731)
XLA Ops:
  0.0 0.9 reshape.14.morton
  0.9 0.0 copy-start
  0.9 1.6 %copy-done = f32[2,1,1,1,512,512]{5,4,3,2,1,0:T(8,128)S(1)} copy-done((f32[2,1,1,1,512,512]{5,4,3,2,1,0:T(8,128)S(1)}, f32[2,1,1,1,512,512]{5,4,3,2,1,0:T(8,128)}, u32[]{:S(2)}) %copy-start) | copy-done | bytes 2097176
  2.4 0.0 copy-start.1
  2.5 0.9 copy-done.1
  3.4 0.0 copy-start.2
  3.4 0.8 copy-done.2
  4.2 0.0 copy-start.3
  4.2 0.7 copy-done.3
  4.8 107.8 %panel_steps.1 = f32[2,512,512]{2,1,0:T(8,128)S(1)} custom-call(f32[2,512,512]{2,1,0:T(8,128)S(1)} %bitcast.6, f32[2,32,512]{2,1,0:T(8,128)S(1)} %copy-done.1, s32[32]{0:T(128)S(1)} %copy-done.3, f32[128,128]{1,0:T(8,128)S(1)} %bitcast.7, s32[32,512]{1,0:T(8,128)S(1)} %reshape.14.morton), custom_call_target="tpu_custom_call" | custom-call | flops 6442450944 | bytes 4194304 | tf_op jit(solution)/shard_map/panel_steps/pallas_call | solution.py:606
  112.7 1.3 %copy.8 = f32[2,1,1,1,512,512]{5,4,3,2,1,0:T(8,128)} copy(f32[2,1,1,1,512,512]{5,4,3,2,1,0:T(8,128)S(1)} %bitcast.5) | data formatting | bytes 4194304
Async XLA Ops:
  0.9 1.6 %copy-start = (f32[2,1,1,1,512,512]{5,4,3,2,1,0:T(8,128)S(1)}, f32[2,1,1,1,512,512]{5,4,3,2,1,0:T(8,128)}, u32[]{:S(2)}) copy-start(f32[2,1,1,1,512,512]{5,4,3,2,1,0:T(8,128)} %param.5) | copy-start | bytes 6291460
  2.4 0.9 copy-start.1
  3.4 0.8 copy-start.2
  4.2 0.7 copy-start.3

commit v2 on v0

v2 whole, which is shorter than its diff:
```python
import jax
import jax.numpy as jnp
from jax import lax
from jax.experimental import pallas as pl
from jax.experimental.pallas import tpu as pltpu
from jax.sharding import PartitionSpec as P

TILE = 512
BLOCK = 128
BLOCKS = TILE // BLOCK
NP = 32
PIECE = 2 * TILE // NP
HALF = PIECE // 2
GROUP = BLOCK // PIECE
ROW_HOP = 4
COL_HOP = 4
CHUNK = TILE // 16
MESH = pl.DeviceIdType.MESH
F32 = jnp.float32
BF16 = jnp.bfloat16


def device(x, y, z, core):
    x, y, z = lax.rem(x + 4, 4), lax.rem(y + 8, 8), lax.rem(z + 8, 8)
    return (z // 4 * 8 + y, x * 8 + z % 4 * 2 + core)


def split(value):
    high = value.astype(BF16)
    return high, (value - high.astype(F32)).astype(BF16)


def dot3(a, b, transposed):
    dims = (((1,), (1 if transposed else 0,)), ((), ()))

    def dot(p, q):
        return lax.dot_general(p, q, dims, preferred_element_type=F32)

    return dot(a[0], b[0]) + (dot(a[0], b[1]) + dot(a[1], b[0]))


def either(*conditions):
    result = conditions[0]
    for condition in conditions[1:]:
        result = result | condition
    return result


def count(*conditions):
    return sum(jnp.where(condition, 1, 0) for condition in conditions)


def kernel(cov, factors, band_in, noise_in, morton_in, out, buf, panel, fac, lead, wide, narrow, band, noise, morton,
           row_got, up_got, down_got, side_got, fac_got, lead_got, one_got,
           z_sent, xp_sent, xm_sent, cross_sent, direct_sent, up_sent, down_sent, side_sent, fac_sent, lead_sent, one_sent,
           local):
    row = lax.axis_index("row")
    col = lax.axis_index("col")
    half, y = row // 8, row % 8
    x, zl, core = col // 8, col % 8 // 2, col % 2
    z = half * 4 + zl
    other = 1 - core
    sibling = device(x, y, z, other)
    home = (x == 0) & (zl == 0)
    away = jnp.logical_not(home)
    first, second = core == 0, core == 1
    low, high = half == 0, half == 1
    tail = high & (y <= 1)
    turn, turn_core = y // 2, y % 2

    back = first & low & (x == 0) & (zl >= 1) & (zl < turn)
    from_below = (zl >= 1) & either(first & high & (x == 0), second & low & (x == 1), second & tail & (x == 2))
    from_xm = either(first & high & (x == 1) & (zl <= turn), second & low & either(x == 2, (x == 1) & (zl == 0)))
    from_xp = either(second & low & (x == 0) & (zl >= 1), second & low & (x == 3) & (zl == 0),
                     second & tail & either((x == 3) & (zl == 0), (x == 2) & (zl == 0), x == 1, (x == 0) & (zl >= 1)))
    row_in = either(back, from_below, from_xm, from_xp)
    z_child = either((zl < 3) & either(first & high & (x == 0), second & low & (x == 1), second & tail & (x == 2)),
                     back & (zl >= 2))
    xp_child = either(first & high & (x == 0) & (zl <= turn), second & low & either(x == 1, home))
    xm_child = either(second & low & either((x == 1) & (zl >= 1), home),
                      second & tail & either(home, (x == 3) & (zl == 0), x == 2, (x == 1) & (zl >= 1)))
    side_out = row_in & jnp.logical_not((x == 3) & low)
    depth_low = jnp.where((x == 1) | (x == 3), zl + 1, zl + 2)
    depth_tail = jnp.where(x == 3, 1, zl + jnp.where(x == 2, 2, jnp.where(x == 1, 3, 4)))
    depths = jnp.where(low, turn - zl + 1, zl + x), jnp.where(low, depth_low, depth_tail)
    depth = jnp.where(first, depths[0], depths[1])

    place = lax.rem(y - 2 * zl - core + 8, 8)
    here = place == 0
    ring = away & (x <= 2)
    source = ring & here
    follower = ring & jnp.logical_not(here)
    turning = source & (x == 0) & low
    own_row = (x == 1) & high & (zl == 0) & (y == 0) & first
    last_out = (x == 3) & (zl == 0) & high & (y == 0) & second
    last_in = (x == 3) & (zl == 0) & high & (y == 1) & first
    last_own = (x == 3) & (zl == 0) & tail & jnp.logical_not(last_in)
    lag = jnp.where(x == 0, 1, jnp.where((x == 1) & low, jnp.where(zl == 0, 2, 1),
                                          jnp.where((x == 2) & high & (zl == 0), 3, 2)))
    held = jnp.where(turning | own_row, 0, jnp.where(last_own, 1, 2))
    send_up = ring & (place <= 6)
    send_down = ring & (place != 1)

    turn_out = home & first & low & (y >= 2)
    cross_home = home & first & (y >= 2)
    cross_near = (x == 1) & (zl == 0) & tail & first
    feed_row = (x == 1) & (zl == 0) & high & first & (y >= 1)
    feed_far = (x == 3) & (zl == 0) & low & second
    direct_out = feed_row | feed_far | last_out
    cross_out = cross_near | (feed_far & (y >= 2))
    jump_out = source & (x == 2) & low & (zl == 0)
    direct_x = jnp.where(last_out, 3, jnp.where(feed_far, 2, 1))
    direct_to = device(direct_x, jnp.where(last_out, 1, y), half * 4 + jnp.where(last_out, 0, turn),
                       jnp.where(last_out, 0, turn_core))
    cross_to = device(jnp.where(feed_far, 2, half), y, (1 - half) * 4 + turn, turn_core)

    fac_own = home & first
    fac_far = (x == 0) & (zl == 3) & second
    fac_next = (x == 1) & (zl == 0) & first
    fac_off = (x == 3) & (zl == 3) & second
    scatter = home & low & (y == 1) & first
    relay = (y == 1) & either(first & ((z == 0) | (z == 7)), second & ((z == 1) | (z == jnp.where(x % 2 == 0, 2, 6))))
    relay_place = core * 8 + x + jnp.where(z == core, 0, 4)

    def relay_chip(number):
        at, near = number % 4, number % 8 < 4
        if number < 8:
            return at, 0 if near else 7
        return at, 1 if near else 2 + 4 * (at % 2)

    def local_copy(number, src, dst):
        return pltpu.make_async_copy(src, dst, local.at[number])

    band_copy = local_copy(0, band_in, band)
    noise_copy = local_copy(1, noise_in, noise)
    morton_copy = local_copy(2, morton_in, morton)
    cov_copy = local_copy(3, cov, out)
    panel_copy = local_copy(4, cov.at[core], panel.at[core])
    band_copy.start()

    @pl.when(home)
    def _():
        panel_copy.start()

    @pl.when(away)
    def _():
        noise_copy.start()
        morton_copy.start()
        cov_copy.start()

    barrier = pltpu.get_barrier_semaphore()

    def greet(target):
        pl.semaphore_signal(barrier, inc=1, device_id=target, device_id_type=MESH)

    def greet_if(condition, target):
        @pl.when(condition)
        def _():
            greet(target)

    greet(sibling)

    @pl.when(home)
    def _():
        for step in range(8):
            @pl.when(first)
            def _():
                @pl.when(y != step)
                def _():
                    greet(device(0, step, z, 0))

                greet(device(1, step, z, 0))

                @pl.when(jnp.logical_not(scatter & (step == 0)))
                def _():
                    at, level = relay_chip(step)
                    greet(device(at, 1, level, 0))

            @pl.when(second)
            def _():
                greet(device(0, step, z + 7, 1))
                greet(device(3, step, z + 7, 1))
                at, level = relay_chip(8 + step)
                greet(device(at, 1, level, 1))

    greet_if(relay & jnp.logical_not(scatter), device(0, 1, 0, 0))
    greet_if(back, device(0, y, z + 1, jnp.where(zl + 1 == turn, turn_core, 0)))
    greet_if(from_below, device(x, y, z + 7, core))
    greet_if(from_xm, device(x + 3, y, z, core))
    greet_if(from_xp, device(x + 1, y, z, core))
    greet_if(follower, device(x, y + 7, z, core))
    greet_if(follower, device(x, y + 1, z, core))
    greet_if(turning, device(0, y, 0, 0))
    greet_if(source & (x == 0) & high, device(0, y, 0, 0))
    greet_if(source & (x == 1) & low, device(jnp.where(zl == 0, 1, 0), y, 4, 0))
    greet_if(source & (x == 1) & high & jnp.logical_not(own_row), device(1, y, 4, 0))
    jump_in = source & (x == 2) & high & (zl == 0)
    greet_if(source & (x == 2) & jnp.logical_not(jump_in), device(3, y, 0, 1))
    greet_if(jump_in, device(2, y, 0, core))
    greet_if(last_in, device(3, 0, 4, 1))
    targets = 1 + count(z_child, xp_child, xm_child, send_up, send_down, turn_out, cross_home, direct_out, cross_out, jump_out,
                        turning & (zl >= 2))
    targets = targets + 7 * count(fac_own) + 8 * count(fac_far, fac_next, fac_off)
    targets = targets + 16 * count(relay) + 14 * count(scatter)
    pl.semaphore_wait(barrier, targets)

    def remote(src, dst, sent, got, target):
        return pltpu.make_async_remote_copy(
            src_ref=src, dst_ref=dst, send_sem=sent, recv_sem=got, device_id=target, device_id_type=MESH
        )

    def total(rows, sent, got):
        return remote(buf.at[0, pl.ds(0, rows)], buf.at[0, pl.ds(0, rows)], sent, got, sibling)

    def chunk_rows(number):
        return pl.ds(pl.multiple_of(number * CHUNK, CHUNK), CHUNK)

    def send_factors(condition, part, target_z, target_core, skip_self):
        @pl.when(condition)
        def _():
            for step in range(8):
                copy = remote(factors.at[part], fac.at[part, chunk_rows(row)], fac_sent, fac_got.at[part],
                              device(0, step, target_z, target_core))
                pl.when(y != step if skip_self else step >= 0)(copy.start)

    own_factor = local_copy(5, factors.at[0], fac.at[0, chunk_rows(row)])
    pl.when(fac_own)(own_factor.start)
    send_factors(fac_own, 0, z, 0, True)
    send_factors(fac_far, 0, z + 1, 1, False)

    own_lead = local_copy(6, cov.at[0, pl.ds(0, CHUNK)], lead.at[pl.ds(0, CHUNK)])

    def scatter_copy(number):
        rows = pl.ds(number * CHUNK, CHUNK)
        at, level = relay_chip(number)
        return remote(cov.at[0, rows], lead.at[rows], one_sent.at[4], one_got.at[4], device(at, 1, level, number // 8))

    @pl.when(scatter)
    def _():
        own_lead.start()
        for number in range(1, 16):
            scatter_copy(number).start()

    side_panel = remote(cov.at[other], panel.at[core], one_sent.at[0], one_got.at[0], sibling)
    pl.when(home)(side_panel.start)
    send_factors(fac_next, 1, z, 0, False)
    send_factors(fac_off, 1, z + 1, 1, False)

    @pl.when(relay)
    def _():
        rows = chunk_rows(relay_place)
        pl.when(scatter)(own_lead.wait)
        arrived = remote(lead.at[rows], lead.at[rows], one_sent.at[4], one_got.at[4], sibling)
        pl.when(jnp.logical_not(scatter))(arrived.wait_recv)
        for number in range(16):
            copy = remote(lead.at[rows], lead.at[rows], lead_sent, lead_got,
                          device(0, number % 8, number // 8 * 4, core))
            pl.when(jnp.logical_not(scatter & (number == 1)))(copy.start)

    def block_rows(number, start=0):
        return pl.ds(pl.multiple_of(start + number * BLOCK, BLOCK), BLOCK)

    def piece(index):
        return pl.ds(pl.multiple_of(index * PIECE, PIECE), PIECE)

    def half_piece(index, which):
        return pl.ds(pl.multiple_of(index * PIECE + which * HALF, HALF), HALF)

    def row_copy(index, sent, target):
        rows = piece(index)
        return remote(buf.at[core, rows], buf.at[core, rows], sent, row_got.at[index], target)

    def side_copy(index, slot):
        rows = piece(index)
        return remote(buf.at[slot, rows], buf.at[slot, rows], side_sent.at[slot], side_got.at[slot, index // (NP // 2)],
                      sibling)

    def source_copy(index, slot, place_to, sent, target):
        rows = piece(index)
        return remote(buf.at[slot, rows], buf.at[place_to, rows], sent, up_got.at[index], target)

    def ring_copy(index, which, sent, got, target):
        rows = half_piece(index, which)
        return remote(buf.at[held, rows], buf.at[2, rows], sent, got.at[index], target)

    z_to = device(x, y, z + jnp.where(back, 7, 1), core)
    xp_to, xm_to = device(x + 1, y, z, core), device(x + 3, y, z, core)
    up_to, down_to = device(x, y + 1, z, core), device(x, y + 7, z, core)

    def send_row(index, to_side):
        def start(condition, copy):
            pl.when(condition)(copy.start)

        start(direct_out, source_copy(index, core, 2, direct_sent, direct_to))
        start(cross_out | cross_home, source_copy(index, core, 2, cross_sent, cross_to))
        start(z_child, row_copy(index, z_sent, z_to))
        start(xm_child, row_copy(index, xm_sent, xm_to))
        start(xp_child, row_copy(index, xp_sent, xp_to))
        start(to_side, side_copy(index, core))

    def side_wait(slot, part):
        total(TILE, side_sent.at[slot], side_got.at[slot, part]).wait_recv()

    def make_panel():
        part_rows = jnp.where(first, half, 1 - half) * 256
        tile_row = core * 16 + row
        side_fac, side_rows = [], pl.ds(pl.multiple_of(part_rows, 256), 256)
        for part in range(2):
            side_fac.append(remote(fac.at[part, side_rows], fac.at[part, side_rows],
                                   one_sent.at[1 + part], one_got.at[1 + part], sibling))
        lead_rows = pl.ds(pl.multiple_of(core * 256, 256), 256)
        side_lead = remote(lead.at[lead_rows], lead.at[lead_rows], one_sent.at[3], one_got.at[3], sibling)

        def split_into(at, load):
            def body(number, carry):
                rows = block_rows(number)
                wide[at, rows], narrow[at, rows] = split(load(rows))
                return carry

            lax.fori_loop(0, BLOCKS, body, 0)

        def send_block(number, start):
            def body(index, carry):
                root_send(start + number * GROUP + index)
                return carry

            lax.fori_loop(0, GROUP, body, 0)

        def root_send(index):
            copy = source_copy(index, 0, 0, direct_sent, device(0, y, turn, turn_core))
            pl.when(turn_out)(copy.start)
            send_row(index, True)

        @pl.when(first)
        def _():
            own_factor.wait()
            total(7 * CHUNK, fac_sent, fac_got.at[0]).wait_recv()

        @pl.when(second)
        def _():
            total(8 * CHUNK, fac_sent, fac_got.at[0]).wait_recv()

        side_fac[0].start()
        band_copy.wait()
        row_band = band[tile_row]
        panel_copy.wait()
        side_panel.wait_recv()
        side_fac[0].wait_recv()
        split_into(0, lambda rows: fac[0, rows])
        kept = (tile_row > 0) & (tile_row <= row_band)

        def first_block(number, carry):
            rows = block_rows(number)
            left = split(jnp.where(kept, panel[0, rows], 0.0))
            buf[core, rows] = dot3(left, (wide[0], narrow[0]), False)
            send_block(number, 0)
            return carry

        lax.fori_loop(0, BLOCKS, first_block, 0)

        def turned_block(number, carry):
            rows = block_rows(number)
            made = dot3(split(buf[core, rows]), (wide[0], narrow[0]), True)
            wide[3, rows], narrow[3, rows] = split(made)
            return carry

        lax.fori_loop(0, BLOCKS, turned_block, 0)
        total(8 * CHUNK, fac_sent, fac_got.at[1]).wait_recv()
        side_fac[1].start()
        pl.when(scatter)(total(7 * CHUNK, lead_sent, lead_got).wait_recv)
        pl.when(jnp.logical_not(scatter))(total(8 * CHUNK, lead_sent, lead_got).wait_recv)
        side_lead.start()
        side_fac[1].wait_recv()
        split_into(1, lambda rows: fac[1, rows])
        lead_kept = band[1] >= 1
        side_lead.wait_recv()
        split_into(2, lambda rows: jnp.where(lead_kept, lead[rows], 0.0))
        panel_kept = (tile_row > 0) & (tile_row - 1 <= row_band)

        def second_block(number, carry):
            rows = block_rows(number)
            update = dot3((wide[3, rows], narrow[3, rows]), (wide[2], narrow[2]), True)
            left = split(jnp.where(panel_kept, panel[1, rows], 0.0) - update)
            made = dot3(left, (wide[1], narrow[1]), False)
            buf[core, block_rows(number, TILE)] = jnp.where(tile_row > 1, made, 0.0)
            send_block(number, NP // 2)
            return carry

        lax.fori_loop(0, BLOCKS, second_block, 0)
        for part in range(2):
            side_wait(other, part)
        for s in range(2):
            def body(number, carry):
                rows = block_rows(number)
                out[s, rows] = buf[s, block_rows(number, core * TILE)]
                return carry

            lax.fori_loop(0, BLOCKS, body, 0)
        side_panel.wait_send()
        side_fac[0].wait_send()
        side_fac[1].wait_send()
        side_lead.wait_send()

        @pl.when(scatter)
        def _():
            total(15 * CHUNK, one_sent.at[4], one_got.at[4]).wait_send()

        pl.when(turn_out)(total(2 * TILE, direct_sent, one_got.at[0]).wait_send)

    def make_base():
        noise_copy.wait()
        morton_copy.wait()
        cov_copy.wait()
        band_copy.wait()
        diagonal = row == lax.rem(col, 16)
        for s in range(2):
            tile = s * 16 + row
            kept = (col <= tile) & (tile - col <= band[tile])
            on_diagonal = diagonal & (col // 16 == s)

            @pl.when(on_diagonal)
            def _():
                turned_noise = noise[...].T
                top = turned_noise.astype(BF16)
                rest = turned_noise - top.astype(F32)
                middle = rest.astype(BF16)
                bottom = (rest - middle.astype(F32)).astype(BF16)
                lanes = lax.broadcasted_iota(jnp.int32, (128, 128), 0)
                for number in range(BLOCKS):
                    stations = morton[pl.ds(tile * BLOCKS + number, 1), :]
                    upper, lower = stations // 128, stations % 128
                    pick = jnp.where(lanes == upper, 1.0, 0.0).astype(BF16)
                    found = jnp.dot(top, pick, preferred_element_type=F32)
                    found = found + (jnp.dot(middle, pick, preferred_element_type=F32)
                                     + jnp.dot(bottom, pick, preferred_element_type=F32))
                    nugget = jnp.sum(jnp.where(lanes == lower, found, 0.0), axis=0, keepdims=True)
                    at = number * BLOCK
                    rows_at = lax.broadcasted_iota(jnp.int32, (BLOCK, TILE), 0) + at
                    cols_at = lax.broadcasted_iota(jnp.int32, (BLOCK, TILE), 1)
                    value = jnp.where(cols_at <= rows_at, out[s, pl.ds(at, BLOCK), :], out[s, :, pl.ds(at, BLOCK)].T)
                    out[s, pl.ds(at, BLOCK), :] = value
                    corner = out[s, pl.ds(at, BLOCK), pl.ds(at, BLOCK)]
                    eye = lanes == lax.broadcasted_iota(jnp.int32, (128, 128), 1)
                    out[s, pl.ds(at, BLOCK), pl.ds(at, BLOCK)] = corner + jnp.where(eye, nugget, 0.0)

            @pl.when(jnp.logical_not(on_diagonal))
            def _():
                def body(number, carry):
                    rows = block_rows(number)
                    out[s, rows] = jnp.where(kept, out[s, rows], 0.0)
                    return carry

                lax.fori_loop(0, BLOCKS, body, 0)

    needed = [away & (col <= s * 16 + row) & (s * 16 + row <= 25) for s in range(2)]
    by_side = [
        away & either(second & either(high & (x == 0), low & (x == 0) & (zl >= 1) & (zl < turn), high & (x == 1) & (zl <= turn),
                                      low & (x == 0) & (zl == turn) & (turn_core == 0)),
                      first & low & (x == 0) & (zl == turn) & (turn_core == 1)),
        away & first & either(low & (x <= 2), tail & either(x <= 2, zl == 0)),
    ]

    def update_block(number):
        part, block = number // BLOCKS, number % BLOCKS

        @pl.when(block == 0)
        def _():
            for s in range(2):
                @pl.when(by_side[s])
                def _():
                    side_wait(s, part)

                @pl.when(needed[s])
                def _():
                    def body(index, carry):
                        rows = block_rows(index)
                        wide[s, rows], narrow[s, rows] = split(buf[s, block_rows(index, part * TILE)])
                        return carry

                    lax.fori_loop(0, BLOCKS, body, 0)

        right = split(buf[held, block_rows(number)])
        columns = pl.ds(pl.multiple_of(block * BLOCK, BLOCK), BLOCK)
        for s in range(2):
            @pl.when(needed[s])
            def _():
                out[s, :, columns] = out[s, :, columns] - dot3((wide[s], narrow[s]), right, True)

    row_delay = depth * ROW_HOP
    col_delay = lag * ROW_HOP
    last_delay = 3 * ROW_HOP
    arrival = jnp.where(ring, col_delay + COL_HOP * jnp.where(here, 0, jnp.maximum(place, 8 - place)), last_delay)
    uses = by_side[0] | turning | (first & row_in), by_side[1] | (second & row_in)
    rows_from = ROW_HOP * jnp.maximum(jnp.where(uses[0], depths[0], 0), jnp.where(uses[1], depths[1], 0))
    update_delay = jnp.maximum(arrival, rows_from + NP // 2 - GROUP + 1)

    def inside(index):
        return (index >= 0) & (index < NP)

    def step(time, carry):
        index = time - row_delay

        @pl.when(row_in & inside(index))
        def _():
            row_copy(index, z_sent, z_to).wait_recv()
            send_row(index, side_out)

        ahead = time - col_delay

        @pl.when(source & inside(ahead))
        def _():
            pl.when(jnp.logical_not(own_row))(source_copy(ahead, 2, 2, up_sent, up_to).wait_recv)

            ring_copy(ahead, 0, up_sent, up_got, up_to).start()
            ring_copy(ahead, 1, down_sent, down_got, down_to).start()

            pl.when(jump_out)(source_copy(ahead, 2, 2, cross_sent, device(2, y, 4, core)).start)

            @pl.when(turning)
            def _():
                side_copy(ahead, 0).start()

                @pl.when(zl >= 2)
                def _():
                    rows = piece(ahead)
                    remote(buf.at[0, rows], buf.at[0, rows], direct_sent, row_got.at[ahead], device(0, y, z + 7, 0)).start()

        going_up = ahead - COL_HOP * place
        going_down = ahead - COL_HOP * (8 - place)
        straight = time - last_delay

        @pl.when(last_in & inside(straight))
        def _():
            source_copy(straight, 2, 2, up_sent, up_to).wait_recv()

        @pl.when(follower & inside(going_up))
        def _():
            copy = ring_copy(going_up, 0, up_sent, up_got, up_to)
            copy.wait_recv()
            pl.when(place <= 6)(copy.start)

        @pl.when(follower & inside(going_down))
        def _():
            copy = ring_copy(going_down, 1, down_sent, down_got, down_to)
            copy.wait_recv()
            pl.when(place >= 2)(copy.start)

        done = time - update_delay + 1

        @pl.when((done > 0) & (done % GROUP == 0) & (done <= NP))
        def _():
            update_block(done // GROUP - 1)

        return carry

    def drain(condition, rows, sent):
        pl.when(condition)(total(rows, sent, one_got.at[0]).wait_send)

    pl.when(home)(make_panel)

    @pl.when(away)
    def _():
        make_base()
        lax.fori_loop(0, update_delay + NP, step, 0)

    drain(z_child, 2 * TILE, z_sent)
    drain(xp_child, 2 * TILE, xp_sent)
    drain(xm_child, 2 * TILE, xm_sent)
    drain(cross_out | cross_home | jump_out, 2 * TILE, cross_sent)
    drain(direct_out | (turning & (zl >= 2)), 2 * TILE, direct_sent)
    drain(send_up, TILE, up_sent)
    drain(send_down, TILE, down_sent)
    for s in range(2):
        drain(either((home | side_out) & (core == s), turning & (s == 0)), 2 * TILE, side_sent.at[s])
    drain(fac_own, 7 * CHUNK, fac_sent)
    drain(fac_far | fac_next | fac_off, 8 * CHUNK, fac_sent)
    drain(relay & scatter, 15 * CHUNK, lead_sent)
    drain(relay & jnp.logical_not(scatter), 16 * CHUNK, lead_sent)


def on_device(cov_tiles, inverse_factors, band, station_noise, morton):
    vmem = pl.BlockSpec(memory_space=pltpu.VMEM)
    hbm = pl.BlockSpec(memory_space=pltpu.HBM)
    dma = pltpu.SemaphoreType.DMA
    out = pl.pallas_call(
        kernel,
        out_shape=jax.ShapeDtypeStruct((2, TILE, TILE), F32),
        in_specs=[hbm] * 5,
        out_specs=vmem,
        scratch_shapes=[
            pltpu.VMEM((3, 2 * TILE, TILE), F32),
            pltpu.VMEM((2, TILE, TILE), F32),
            pltpu.VMEM((2, TILE, TILE), F32),
            pltpu.VMEM((TILE, TILE), F32),
            pltpu.VMEM((4, TILE, TILE), BF16),
            pltpu.VMEM((4, TILE, TILE), BF16),
            pltpu.SMEM((32,), jnp.int32),
            pltpu.VMEM((128, 128), F32),
            pltpu.VMEM((128, 128), jnp.int32),
            dma((NP,)), dma((NP,)), dma((NP,)), dma((2, 2)), dma((2,)), dma, dma((5,)),
            dma, dma, dma, dma, dma, dma, dma, dma((2,)), dma, dma, dma((5,)),
            dma((7,)),
        ],
        compiler_params=pltpu.CompilerParams(
            collective_id=0, has_side_effects=True, vmem_limit_bytes=40 * 1024 * 1024
        ),
        cost_estimate=pl.CostEstimate(flops=6 * 4 * 2 * TILE**3, bytes_accessed=4 * 1024 * 1024, transcendentals=0),
        name="panel_steps",
    )(
        cov_tiles.reshape(2, TILE, TILE),
        inverse_factors,
        band,
        station_noise.reshape(128, 128),
        morton.reshape(128, 128),
    )
    return out.reshape(cov_tiles.shape)


def solution(mesh):
    placed = (P(None, "row", None, "col", None, None), P(None, "row", None), P(), P(), P())
    return jax.shard_map(
        on_device,
        mesh=mesh,
        in_specs=placed,
        out_specs=P(None, "row", None, "col", None, None),
        check_vma=False,
    )
```

time: 1190 us -> 87.4 us (0.07)
  the two profiles are of different devices: /device:TPU:2 before, /device:TPU:10 now
where the time goes in v2:
time: 87.4 us; the launch traced here: 87.1 us
  Pallas kernels  81 us (93%)
  local copies, waits for them, and re-layouts  6.15 us (7%)
    pallas_call x1, Pallas kernels, on_device(): pl.pallas_call(kernel, out_shape=jax.ShapeDtypeStruct((2, TILE, TILE), F3...  81 us
    unnamed x11, local copies, waits for them, and re-layouts  6.15 us

profile of v2, /device:TPU:10, one launch (start us, length us, event | category | flops | bytes accessed | tf_op | source)
XLA Modules:
  0.0 87.1 jit_solution(2864189647417932680)
XLA Ops:
  0.0 0.0 copy-start
  0.0 1.6 %copy-done = f32[2,1,1,1,512,512]{5,4,3,2,1,0:T(8,128)S(1)} copy-done((f32[2,1,1,1,512,512]{5,4,3,2,1,0:T(8,128)S(1)}, f32[2,1,1,1,512,512]{5,4,3,2,1,0:T(8,128)}, u32[]{:S(2)}) %copy-start) | copy-done | bytes 2097176
  1.6 0.0 copy-start.1
  1.6 0.9 %copy-done.1 = f32[2,32,512]{2,1,0:T(8,128)S(1)} copy-done((f32[2,32,512]{2,1,0:T(8,128)S(1)}, f32[2,32,512]{2,1,0:T(8,128)}, u32[]{:S(2)}) %copy-start.1) | copy-done | bytes 131096
  2.5 0.0 copy-start.2
  2.5 0.8 copy-done.2
  3.3 0.0 copy-start.3
  3.3 0.8 copy-done.3
  4.2 0.0 copy-start.4
  4.2 0.7 copy-done.4
  4.8 81.0 %panel_steps.1 = f32[2,512,512]{2,1,0:T(8,128)S(1)} custom-call(f32[2,512,512]{2,1,0:T(8,128)S(1)} %bitcast.7, f32[2,32,512]{2,1,0:T(8,128)S(1)} %copy-done.1, s32[32]{0:T(128)S(1)} %copy-done.4, f32[128,128]{1,0:T(8,128)S(1)} %bitcast.8, s32[128,128]{1,0:T(8,128)S(1)} %bitcast.9), custom_call_target="tpu_custom_call" | custom-call | flops 6442450944 | bytes 4194304 | tf_op jit(solution)/shard_map/panel_steps/pallas_call | solution.py:585
  85.8 1.3 %copy.8 = f32[2,1,1,1,512,512]{5,4,3,2,1,0:T(8,128)} copy(f32[2,1,1,1,512,512]{5,4,3,2,1,0:T(8,128)S(1)} %bitcast.6) | data formatting | bytes 4194304
Async XLA Ops:
  0.0 1.6 %copy-start = (f32[2,1,1,1,512,512]{5,4,3,2,1,0:T(8,128)S(1)}, f32[2,1,1,1,512,512]{5,4,3,2,1,0:T(8,128)}, u32[]{:S(2)}) copy-start(f32[2,1,1,1,512,512]{5,4,3,2,1,0:T(8,128)} %param.5) | copy-start | bytes 6291460
  1.6 0.9 %copy-start.1 = (f32[2,32,512]{2,1,0:T(8,128)S(1)}, f32[2,32,512]{2,1,0:T(8,128)}, u32[]{:S(2)}) copy-start(f32[2,32,512]{2,1,0:T(8,128)} %factors.1) | copy-start | bytes 393220
  2.5 0.8 copy-start.2
  3.3 0.8 copy-start.3
  4.2 0.7 copy-start.4

commit v3 on v2

--- a/solution.py
+++ b/solution.py
@@ -13,7 +13,10 @@
 HALF = PIECE // 2
 GROUP = BLOCK // PIECE
 ROW_HOP = 4
-COL_HOP = 4
+COL_HOP = 5
+TIP = 4
+BULK = NP - TIP
+SLACK = 8
 CHUNK = TILE // 16
 MESH = pl.DeviceIdType.MESH
 F32 = jnp.float32
@@ -53,7 +56,7 @@
 def kernel(cov, factors, band_in, noise_in, morton_in, out, buf, panel, fac, lead, wide, narrow, band, noise, morton,
            row_got, up_got, down_got, side_got, fac_got, lead_got, one_got,
            z_sent, xp_sent, xm_sent, cross_sent, direct_sent, up_sent, down_sent, side_sent, fac_sent, lead_sent, one_sent,
-           local):
+           tip_sent, local):
     row = lax.axis_index("row")
     col = lax.axis_index("col")
     half, y = row // 8, row % 8
@@ -100,6 +103,8 @@
     held = jnp.where(turning | own_row, 0, jnp.where(last_own, 1, 2))
     send_up = ring & (place <= 6)
     send_down = ring & (place != 1)
+    tip_up = ring & (place <= 3)
+    tip_down = ring & (here | (place >= 6))
 
     turn_out = home & first & low & (y >= 2)
     cross_home = home & first & (y >= 2)
@@ -114,19 +119,16 @@
                        jnp.where(last_out, 0, turn_core))
     cross_to = device(jnp.where(feed_far, 2, half), y, (1 - half) * 4 + turn, turn_core)
 
-    fac_own = home & first
+    fac_own = home & second
     fac_far = (x == 0) & (zl == 3) & second
     fac_next = (x == 1) & (zl == 0) & first
     fac_off = (x == 3) & (zl == 3) & second
     scatter = home & low & (y == 1) & first
-    relay = (y == 1) & either(first & ((z == 0) | (z == 7)), second & ((z == 1) | (z == jnp.where(x % 2 == 0, 2, 6))))
-    relay_place = core * 8 + x + jnp.where(z == core, 0, 4)
+    relay = (y == 1) & either(first & ((z == 7) | (z == 2)), second & ((z == 1) | (z == 6)))
+    relay_place = core * 8 + x + jnp.where((z == 7) | (z == 1), 0, 4)
 
     def relay_chip(number):
-        at, near = number % 4, number % 8 < 4
-        if number < 8:
-            return at, 0 if near else 7
-        return at, 1 if near else 2 + 4 * (at % 2)
+        return number % 4, (7, 2, 1, 6)[number // 4]
 
     def local_copy(number, src, dst):
         return pltpu.make_async_copy(src, dst, local.at[number])
@@ -165,16 +167,10 @@
         for step in range(8):
             @pl.when(first)
             def _():
-                @pl.when(y != step)
-                def _():
-                    greet(device(0, step, z, 0))
-
+                greet(device(0, step, z, 1))
                 greet(device(1, step, z, 0))
-
-                @pl.when(jnp.logical_not(scatter & (step == 0)))
-                def _():
-                    at, level = relay_chip(step)
-                    greet(device(at, 1, level, 0))
+                at, level = relay_chip(step)
+                greet(device(at, 1, level, 0))
 
             @pl.when(second)
             def _():
@@ -183,7 +179,7 @@
                 at, level = relay_chip(8 + step)
                 greet(device(at, 1, level, 1))
 
-    greet_if(relay & jnp.logical_not(scatter), device(0, 1, 0, 0))
+    greet_if(relay, device(0, 1, 0, 0))
     greet_if(back, device(0, y, z + 1, jnp.where(zl + 1 == turn, turn_core, 0)))
     greet_if(from_below, device(x, y, z + 7, core))
     greet_if(from_xm, device(x + 3, y, z, core))
@@ -200,8 +196,7 @@
     greet_if(last_in, device(3, 0, 4, 1))
     targets = 1 + count(z_child, xp_child, xm_child, send_up, send_down, turn_out, cross_home, direct_out, cross_out, jump_out,
                         turning & (zl >= 2))
-    targets = targets + 7 * count(fac_own) + 8 * count(fac_far, fac_next, fac_off)
-    targets = targets + 16 * count(relay) + 14 * count(scatter)
+    targets = targets + 8 * count(fac_own, fac_far, fac_next, fac_off) + 16 * count(relay, scatter)
     pl.semaphore_wait(barrier, targets)
 
     def remote(src, dst, sent, got, target):
@@ -215,20 +210,23 @@
     def chunk_rows(number):
         return pl.ds(pl.multiple_of(number * CHUNK, CHUNK), CHUNK)
 
-    def send_factors(condition, part, target_z, target_core, skip_self):
+    def send_factors(condition, part, which, target_z, target_core):
+        rows = pl.ds(which * (CHUNK // 2), CHUNK // 2)
+        there = pl.ds(pl.multiple_of(row * CHUNK + which * (CHUNK // 2), CHUNK // 2), CHUNK // 2)
+
         @pl.when(condition)
         def _():
             for step in range(8):
-                copy = remote(factors.at[part], fac.at[part, chunk_rows(row)], fac_sent, fac_got.at[part],
-                              device(0, step, target_z, target_core))
-                pl.when(y != step if skip_self else step >= 0)(copy.start)
-
-    own_factor = local_copy(5, factors.at[0], fac.at[0, chunk_rows(row)])
-    pl.when(fac_own)(own_factor.start)
-    send_factors(fac_own, 0, z, 0, True)
-    send_factors(fac_far, 0, z + 1, 1, False)
-
-    own_lead = local_copy(6, cov.at[0, pl.ds(0, CHUNK)], lead.at[pl.ds(0, CHUNK)])
+                remote(factors.at[part, rows], fac.at[part, there], fac_sent, fac_got.at[part],
+                       device(0, step, target_z, target_core)).start()
+
+    def send_part(part):
+        send_factors(fac_own, part, 0, z, 0)
+        send_factors(fac_next, part, 1, z, 0)
+        send_factors(fac_far, part, 0, z + 1, 1)
+        send_factors(fac_off, part, 1, z + 1, 1)
+
+    send_part(0)
 
     def scatter_copy(number):
         rows = pl.ds(number * CHUNK, CHUNK)
@@ -237,25 +235,20 @@
 
     @pl.when(scatter)
     def _():
-        own_lead.start()
-        for number in range(1, 16):
+        for number in range(16):
             scatter_copy(number).start()
 
     side_panel = remote(cov.at[other], panel.at[core], one_sent.at[0], one_got.at[0], sibling)
     pl.when(home)(side_panel.start)
-    send_factors(fac_next, 1, z, 0, False)
-    send_factors(fac_off, 1, z + 1, 1, False)
+    send_part(1)
 
     @pl.when(relay)
     def _():
         rows = chunk_rows(relay_place)
-        pl.when(scatter)(own_lead.wait)
-        arrived = remote(lead.at[rows], lead.at[rows], one_sent.at[4], one_got.at[4], sibling)
-        pl.when(jnp.logical_not(scatter))(arrived.wait_recv)
+        remote(lead.at[rows], lead.at[rows], one_sent.at[4], one_got.at[4], sibling).wait_recv()
         for number in range(16):
-            copy = remote(lead.at[rows], lead.at[rows], lead_sent, lead_got,
-                          device(0, number % 8, number // 8 * 4, core))
-            pl.when(jnp.logical_not(scatter & (number == 1)))(copy.start)
+            remote(lead.at[rows], lead.at[rows], lead_sent, lead_got,
+                   device(0, number % 8, number // 8 * 4, core)).start()
 
     def block_rows(number, start=0):
         return pl.ds(pl.multiple_of(start + number * BLOCK, BLOCK), BLOCK)
@@ -278,6 +271,10 @@
     def source_copy(index, slot, place_to, sent, target):
         rows = piece(index)
         return remote(buf.at[slot, rows], buf.at[place_to, rows], sent, up_got.at[index], target)
+
+    def tip_copy(index, which, got, target):
+        rows = piece(index)
+        return remote(buf.at[held, rows], buf.at[2, rows], tip_sent.at[which], got.at[index], target)
 
     def ring_copy(index, which, sent, got, target):
         rows = half_piece(index, which)
@@ -331,15 +328,7 @@
             pl.when(turn_out)(copy.start)
             send_row(index, True)
 
-        @pl.when(first)
-        def _():
-            own_factor.wait()
-            total(7 * CHUNK, fac_sent, fac_got.at[0]).wait_recv()
-
-        @pl.when(second)
-        def _():
-            total(8 * CHUNK, fac_sent, fac_got.at[0]).wait_recv()
-
+        total(8 * CHUNK, fac_sent, fac_got.at[0]).wait_recv()
         side_fac[0].start()
         band_copy.wait()
         row_band = band[tile_row]
@@ -367,8 +356,7 @@
         lax.fori_loop(0, BLOCKS, turned_block, 0)
         total(8 * CHUNK, fac_sent, fac_got.at[1]).wait_recv()
         side_fac[1].start()
-        pl.when(scatter)(total(7 * CHUNK, lead_sent, lead_got).wait_recv)
-        pl.when(jnp.logical_not(scatter))(total(8 * CHUNK, lead_sent, lead_got).wait_recv)
+        total(8 * CHUNK, lead_sent, lead_got).wait_recv()
         side_lead.start()
         side_fac[1].wait_recv()
         split_into(1, lambda rows: fac[1, rows])
@@ -403,7 +391,7 @@
 
         @pl.when(scatter)
         def _():
-            total(15 * CHUNK, one_sent.at[4], one_got.at[4]).wait_send()
+            total(16 * CHUNK, one_sent.at[4], one_got.at[4]).wait_send()
 
         pl.when(turn_out)(total(2 * TILE, direct_sent, one_got.at[0]).wait_send)
 
@@ -492,11 +480,14 @@
     arrival = jnp.where(ring, col_delay + COL_HOP * jnp.where(here, 0, jnp.maximum(place, 8 - place)), last_delay)
     uses = by_side[0] | turning | (first & row_in), by_side[1] | (second & row_in)
     rows_from = ROW_HOP * jnp.maximum(jnp.where(uses[0], depths[0], 0), jnp.where(uses[1], depths[1], 0))
-    update_delay = jnp.maximum(arrival, rows_from + NP // 2 - GROUP + 1)
+    update_delay = jnp.maximum(arrival, rows_from + SLACK + NP // 2 - GROUP + 1)
 
     def inside(index):
         return (index >= 0) & (index < NP)
 
+    def in_bulk(index):
+        return (index >= 0) & (index < BULK)
+
     def step(time, carry):
         index = time - row_delay
 
@@ -511,8 +502,15 @@
         def _():
             pl.when(jnp.logical_not(own_row))(source_copy(ahead, 2, 2, up_sent, up_to).wait_recv)
 
-            ring_copy(ahead, 0, up_sent, up_got, up_to).start()
-            ring_copy(ahead, 1, down_sent, down_got, down_to).start()
+            @pl.when(ahead < BULK)
+            def _():
+                ring_copy(ahead, 0, up_sent, up_got, up_to).start()
+                ring_copy(ahead, 1, down_sent, down_got, down_to).start()
+
+            @pl.when(ahead >= BULK)
+            def _():
+                tip_copy(ahead, 0, up_got, up_to).start()
+                tip_copy(ahead, 1, down_got, down_to).start()
 
             pl.when(jump_out)(source_copy(ahead, 2, 2, cross_sent, device(2, y, 4, core)).start)
 
@@ -533,13 +531,25 @@
         def _():
             source_copy(straight, 2, 2, up_sent, up_to).wait_recv()
 
-        @pl.when(follower & inside(going_up))
+        @pl.when(follower & (place <= 4) & (going_up >= BULK) & (going_up < NP))
+        def _():
+            copy = tip_copy(going_up, 0, up_got, up_to)
+            copy.wait_recv()
+            pl.when(place <= 3)(copy.start)
+
+        @pl.when(follower & (place >= 5) & (going_down >= BULK) & (going_down < NP))
+        def _():
+            copy = tip_copy(going_down, 1, down_got, down_to)
+            copy.wait_recv()
+            pl.when(place >= 6)(copy.start)
+
+        @pl.when(follower & in_bulk(going_up))
         def _():
             copy = ring_copy(going_up, 0, up_sent, up_got, up_to)
             copy.wait_recv()
             pl.when(place <= 6)(copy.start)
 
-        @pl.when(follower & inside(going_down))
+        @pl.when(follower & in_bulk(going_down))
         def _():
             copy = ring_copy(going_down, 1, down_sent, down_got, down_to)
             copy.wait_recv()
@@ -568,14 +578,14 @@
     drain(xm_child, 2 * TILE, xm_sent)
     drain(cross_out | cross_home | jump_out, 2 * TILE, cross_sent)
     drain(direct_out | (turning & (zl >= 2)), 2 * TILE, direct_sent)
-    drain(send_up, TILE, up_sent)
-    drain(send_down, TILE, down_sent)
+    drain(send_up, BULK * HALF, up_sent)
+    drain(send_down, BULK * HALF, down_sent)
+    drain(tip_up, TIP * PIECE, tip_sent.at[0])
+    drain(tip_down, TIP * PIECE, tip_sent.at[1])
     for s in range(2):
         drain(either((home | side_out) & (core == s), turning & (s == 0)), 2 * TILE, side_sent.at[s])
-    drain(fac_own, 7 * CHUNK, fac_sent)
-    drain(fac_far | fac_next | fac_off, 8 * CHUNK, fac_sent)
-    drain(relay & scatter, 15 * CHUNK, lead_sent)
-    drain(relay & jnp.logical_not(scatter), 16 * CHUNK, lead_sent)
+    drain(either(fac_own, fac_far, fac_next, fac_off), 8 * CHUNK, fac_sent)
+    drain(relay, 16 * CHUNK, lead_sent)
 
 
 def on_device(cov_tiles, inverse_factors, band, station_noise, morton):
@@ -599,7 +609,7 @@
             pltpu.VMEM((128, 128), jnp.int32),
             dma((NP,)), dma((NP,)), dma((NP,)), dma((2, 2)), dma((2,)), dma, dma((5,)),
             dma, dma, dma, dma, dma, dma, dma, dma((2,)), dma, dma, dma((5,)),
-            dma((7,)),
+            dma((2,)), dma((5,)),
         ],
         compiler_params=pltpu.CompilerParams(
             collective_id=0, has_side_effects=True, vmem_limit_bytes=40 * 1024 * 1024
@@ -607,11 +617,16 @@
         cost_estimate=pl.CostEstimate(flops=6 * 4 * 2 * TILE**3, bytes_accessed=4 * 1024 * 1024, transcendentals=0),
         name="panel_steps",
     )(
-        cov_tiles.reshape(2, TILE, TILE),
-        inverse_factors,
-        band,
-        station_noise.reshape(128, 128),
-        morton.reshape(128, 128),
+        *(
+            pltpu.with_memory_space_constraint(operand, pltpu.HBM)
+            for operand in (
+                cov_tiles.reshape(2, TILE, TILE),
+                inverse_factors,
+                band,
+                station_noise.reshape(128, 128),
+                morton.reshape(128, 128),
+            )
+        )
     )
     return out.reshape(cov_tiles.shape)
 

time: 87.4 us -> 80.1 us (0.916)
  local copies, waits for them, and re-layouts: 6.15 us -> 1.32 us
  Pallas kernels: 81 us -> 78.6 us
    unnamed x11 -> x1, local copies, waits for them, and re-layouts: 6.15 us -> 1.32 us
    pallas_call x1, Pallas kernels: 81 us -> 78.6 us  [on_device(): pl.pallas_call(kernel, out_shape=jax.ShapeDtypeStruct((2, TILE, TILE), F3...]
where the time goes in v3:
time: 80.1 us; the launch traced here: 80 us
  Pallas kernels  78.6 us (98%)
  local copies, waits for them, and re-layouts  1.32 us (2%)
    pallas_call x1, Pallas kernels, on_device(): pl.pallas_call(kernel, out_shape=jax.ShapeDtypeStruct((2, TILE, TILE), F3...  78.6 us

profile of v3, /device:TPU:10, one launch (start us, length us, event | category | flops | bytes accessed | tf_op | source)
XLA Modules:
  0.0 80.0 jit_solution(9982311337001148739)
XLA Ops:
  0.0 78.6 %panel_steps.1 = f32[2,512,512]{2,1,0:T(8,128)S(1)} custom-call(f32[2,512,512]{2,1,0:T(8,128)} %bitcast.7, f32[2,32,512]{2,1,0:T(8,128)} %factors.1, s32[32]{0:T(128)} %band_in.1, f32[128,128]{1,0:T(8,128)} %bitcast.8, s32[128,128]{1,0:T(8,128)} %bitcast.9), custom_call_target="tpu_custom_call" | custom-call | flops 6442450944 | bytes 4194304 | tf_op jit(solution)/shard_map/panel_steps/pallas_call | solution.py:595
  78.6 1.3 %copy.8 = f32[2,1,1,1,512,512]{5,4,3,2,1,0:T(8,128)} copy(f32[2,1,1,1,512,512]{5,4,3,2,1,0:T(8,128)S(1)} %bitcast.6) | data formatting | bytes 4194304

commit v4 on v3

--- a/solution.py
+++ b/solution.py
@@ -8,15 +8,15 @@
 TILE = 512
 BLOCK = 128
 BLOCKS = TILE // BLOCK
-NP = 32
+NP = 64
 PIECE = 2 * TILE // NP
 HALF = PIECE // 2
 GROUP = BLOCK // PIECE
-ROW_HOP = 4
-COL_HOP = 5
-TIP = 4
+ROW_HOP = 8
+COL_HOP = 10
+TIP = 8
 BULK = NP - TIP
-SLACK = 8
+SLACK = 16
 CHUNK = TILE // 16
 MESH = pl.DeviceIdType.MESH
 F32 = jnp.float32
@@ -326,7 +326,7 @@
         def root_send(index):
             copy = source_copy(index, 0, 0, direct_sent, device(0, y, turn, turn_core))
             pl.when(turn_out)(copy.start)
-            send_row(index, True)
+            send_row(index, False)
 
         total(8 * CHUNK, fac_sent, fac_got.at[0]).wait_recv()
         side_fac[0].start()
@@ -375,6 +375,9 @@
             return carry
 
         lax.fori_loop(0, BLOCKS, second_block, 0)
+        for part in range(2):
+            rows = pl.ds(part * TILE, TILE)
+            remote(buf.at[core, rows], buf.at[core, rows], side_sent.at[core], side_got.at[core, part], sibling).start()
         for part in range(2):
             side_wait(other, part)
         for s in range(2):

time: 80.1 us -> 79.5 us (level)
  no operation moved by 1% of the time
where the time goes in v4:
time: 79.5 us; the launch traced here: 79.4 us
  Pallas kernels  78 us (98%)
  local copies, waits for them, and re-layouts  1.32 us (2%)
    pallas_call x1, Pallas kernels, on_device(): pl.pallas_call(kernel, out_shape=jax.ShapeDtypeStruct((2, TILE, TILE), F3...  78 us

profile of v4, /device:TPU:10, one launch (start us, length us, event | category | flops | bytes accessed | tf_op | source)
XLA Modules:
  0.0 79.4 jit_solution(9979171006665271031)
XLA Ops:
  0.0 78.0 %panel_steps.1 = f32[2,512,512]{2,1,0:T(8,128)S(1)} custom-call(f32[2,512,512]{2,1,0:T(8,128)} %bitcast.7, f32[2,32,512]{2,1,0:T(8,128)} %factors.1, s32[32]{0:T(128)} %band_in.1, f32[128,128]{1,0:T(8,128)} %bitcast.8, s32[128,128]{1,0:T(8,128)} %bitcast.9), custom_call_target="tpu_custom_call" | custom-call | flops 6442450944 | bytes 4194304 | tf_op jit(solution)/shard_map/panel_steps/pallas_call | solution.py:598
  78.0 1.3 %copy.8 = f32[2,1,1,1,512,512]{5,4,3,2,1,0:T(8,128)} copy(f32[2,1,1,1,512,512]{5,4,3,2,1,0:T(8,128)S(1)} %bitcast.6) | data formatting | bytes 4194304
